TPU v7x, 32 devices: a whole 2x2x4 slice. The times are simulated.
32 devices in a mesh: dp: 16 (over z, y, core), tensor: 2 (over x).
Axes of the slice: x: 2, y: 2, z: 4, core: 2. Of those that a mesh axis runs over, the one named last changes fastest.
Arguments:
- layer_inputs: bfloat16 [2048, 8192], P('dp', 'tensor'), may hold values from -6 to 6
- out_grads: bfloat16 [2048, 14336], P('dp', 'tensor'), may hold values from -0.125 to 0.125
- basis: float32 [8192, 512], P('tensor'), may hold values from -0.0625 to 0.0625
- first: float32 [512, 14336], P('dp', 'tensor'), may hold values from -3 to 3
- second: float32 [512, 14336], P('dp', 'tensor'), may hold values from 0.05 to 2
Outputs:
- new_basis: float32 [8192, 512], P('tensor')
- new_first: float32 [512, 14336], P('dp', 'tensor')
- new_second: float32 [512, 14336], P('dp', 'tensor')
- update: float32 [512, 14336], P('dp', 'tensor')
All inputs are finite; a program needn't handle non-finite values.
Results may differ from a plain program's by a relative error of at most 0.0013.
The roundings to bfloat16 on the way count: a program that leaves them out, or rounds other values in their place, can miss the bound.
Values may be sent and summed in bfloat16 or wider, within the bound.
A program may use at most 128 MiB of HBM per device.

v0:
```python
import jax
import jax.numpy as jnp
from jax import lax
from jax.sharding import PartitionSpec as P

PI_STEPS = 6


EXACT = lax.Precision.HIGHEST


def matmul(left, right):
    return jnp.dot(left, right, precision=EXACT, preferred_element_type=jnp.float32)


def leading(normed):
    rank_count = normed.shape[0]
    vector = jnp.ones((rank_count,), jnp.float32) / jnp.sqrt(jnp.float32(rank_count))
    for sweep in range(PI_STEPS):
        vector = matmul(normed, vector)
        vector = vector / jnp.sqrt(jnp.sum(vector * vector) + 1e-12)
    return vector


def adam_step(rotated_m, rotated_v, grad_new):
    new_first = 0.9 * rotated_m + 0.1 * grad_new
    new_second = 0.95 * rotated_v + 0.05 * grad_new * grad_new
    update = new_first / (jnp.sqrt(new_second) + 1e-06)
    return (new_first, new_second, update)


def merged_kernel(coupling, correlation, square):
    cross = matmul(coupling.T, coupling)
    return square - 2.0 * cross + matmul(coupling.T, matmul(correlation, coupling))


def merged_rotation(coupling, correlation, vector, sigma, cosine_val, sine_val):
    lifted = matmul(coupling, vector)
    left_over = (lifted - matmul(correlation.T, lifted)) / sigma
    return (
        correlation
        + (cosine_val - 1.0) * jnp.outer(vector, matmul(correlation.T, vector))
        + sine_val * jnp.outer(vector, left_over)
    )


def body(layer_inputs, out_grads, basis, first, second):
    basis_low = basis.astype(jnp.bfloat16)
    score_part = jnp.dot(layer_inputs, basis_low, preferred_element_type=jnp.float32)
    scores = lax.psum(score_part, "tensor").astype(jnp.bfloat16)
    grad_part = jnp.dot(scores.T, out_grads, preferred_element_type=jnp.float32)
    grad_own = lax.psum_scatter(grad_part, "dp", scatter_dimension=0, tiled=True)
    grad_low = lax.all_gather(grad_own.astype(jnp.bfloat16), "dp", axis=0, tiled=True)
    back_part = jnp.dot(out_grads, grad_low.T, preferred_element_type=jnp.float32)
    backward = lax.psum(back_part, "tensor").astype(jnp.bfloat16)
    tangent_part = jnp.dot(layer_inputs.T, backward, preferred_element_type=jnp.float32)
    tangent = lax.psum(tangent_part, "dp")
    coupling, correlation, square = lax.psum(
        (matmul(basis.T, tangent), matmul(basis.T, basis), matmul(tangent.T, tangent)), "tensor"
    )
    resid_rows = tangent - matmul(basis, coupling)
    kernel = merged_kernel(coupling, correlation, square)
    total = jnp.trace(kernel)
    normed = kernel / total
    vector = leading(normed)
    ratio = jnp.sum(vector * matmul(normed, vector))
    theta = 4.0 * jnp.sqrt(ratio)
    sigma = jnp.sqrt(total * ratio + 1e-06)
    left_part = matmul(resid_rows, vector) / sigma
    cosine_val = jnp.cos(theta)
    sine_val = jnp.sin(theta)
    basis_dir = matmul(basis, vector)
    new_basis = (
        basis
        + (cosine_val - 1.0) * jnp.outer(basis_dir, vector)
        + sine_val * jnp.outer(left_part, vector)
    )
    rotation = merged_rotation(coupling, correlation, vector, sigma, cosine_val, sine_val)
    left_low = left_part.astype(jnp.bfloat16)
    probe_part = jnp.dot(layer_inputs, left_low, preferred_element_type=jnp.float32)
    probe = lax.psum(probe_part, "tensor").astype(jnp.bfloat16)
    rows_own = first.shape[0]
    row_start = lax.axis_index("dp") * rows_own
    vector_own = lax.dynamic_slice_in_dim(vector, row_start, rows_own, 0)
    along_part = jnp.dot(probe, out_grads, preferred_element_type=jnp.float32)
    lead_part = matmul(vector_own, grad_own)
    along, lead_row = lax.psum((along_part, lead_part), "dp")
    rot_own = lax.dynamic_slice_in_dim(rotation, row_start, rows_own, 0)
    rot_square = rot_own * rot_own
    empty = jnp.zeros(first.shape, jnp.float32)
    pieces = (
        lax.all_gather(first, "dp", axis=0, tiled=True),
        lax.all_gather(second, "dp", axis=0, tiled=True),
    )
    count = pieces[0].shape[0]
    cols_m = lax.slice_in_dim(rot_own, 0, count, axis=1)
    cols_v = lax.slice_in_dim(rot_square, 0, count, axis=1)
    rotated_m = empty + matmul(cols_m, pieces[0])
    rotated_v = empty + matmul(cols_v, pieces[1])
    grad_new = (
        grad_own
        + (cosine_val - 1.0) * jnp.outer(vector_own, lead_row)
        + sine_val * jnp.outer(vector_own, along)
    )
    new_first, new_second, update = adam_step(rotated_m, rotated_v, grad_new)
    return (new_basis, new_first, new_second, update)


def solution(mesh):
    return jax.shard_map(
        body,
        mesh=mesh,
        in_specs=(
            P("dp", "tensor"),
            P("dp", "tensor"),
            P("tensor", None),
            P("dp", "tensor"),
            P("dp", "tensor"),
        ),
        out_specs=(P("tensor", None), P("dp", "tensor"), P("dp", "tensor"), P("dp", "tensor")),
        check_vma=False,
    )
```

profile of v0, /device:TPU:13, one launch (start us, length us, event | category | flops | bytes accessed | tf_op | source)
XLA Modules:
  0.0 807.6 jit_solution(2881724036879555296)
XLA Ops:
  7.2 4.5 fusion.3
  11.8 9.8 %all-reduce.10 = bf16[128,512]{1,0:T(8,128)(2,1)S(1)} all-reduce(f32[128,512]{1,0:T(8,128)S(1)} %fusion.3), channel_id=1, replica_groups=mesh['dp'=16,'tensor'=2] {'tensor'}, use_global_device_ids=true, to_apply=%region_0.0 | all-reduce | flops 65536 | bytes 393216 | tf_op jit(solution)/shard_map/psum | solution.py:50
  21.6 7.3 fusion.51
  29.0 150.5 %reduce-scatter.2.cloned.1.call-done = f32[32,7168]{1,0:T(8,128)} async-done(((f32[512,7168]{1,0:T(8,128)}), f32[32,7168]{1,0:T(8,128)}) %reduce-scatter.2.cloned.1.call-update) | async-done | bytes 917520 | tf_op jit(solution)/shard_map/reduce_scatter | solution.py:52
  181.6 68.6 %all-gather.4.cloned.1.call-done = bf16[512,7168]{1,0:T(8,128)(2,1)} async-done(((bf16[32,7168]{1,0:T(8,128)(2,1)}), bf16[512,7168]{1,0:T(8,128)(2,1)}) %all-gather.4.cloned.1.call-update) | async-done | bytes 7340048 | tf_op jit(solution)/shard_map/all_gather | solution.py:53
  250.1 5.1 convolution_bitcast_fusion.2
  255.3 10.7 %all-reduce.11 = bf16[128,512]{0,1:T(8,128)(2,1)S(1)} all-reduce(f32[128,512]{0,1:T(8,128)S(1)} %convolution_bitcast_fusion.2), channel_id=1, replica_groups=mesh['dp'=16,'tensor'=2] {'tensor'}, use_global_device_ids=true, to_apply=%region_2.0 | all-reduce | flops 65536 | bytes 393216 | tf_op jit(solution)/shard_map/psum | solution.py:55
  266.0 4.6 convolution_bitcast_fusion
  270.9 18.3 %fusion.40 = f32[512,512]{1,0:T(8,128)} fusion(f32[4096,512]{1,0:T(8,128)} %param.7), kind=kOutput, calls=%fused_computation.70 | convolution fusion | flops 12884901888 | bytes 9437184 | tf_op jit(solution)/shard_map/dot_general | solution.py:13
  289.1 151.0 %all-reduce.7.cloned.1.call-done = f32[4096,512]{0,1:T(8,128)} async-done(((f32[4096,512]{0,1:T(8,128)}), f32[4096,512]{0,1:T(8,128)}) %all-reduce.7.cloned.1.call-update) | async-done | bytes 8388624 | tf_op jit(solution)/shard_map/psum | solution.py:57
  440.1 17.4 %convolution_bitcast_fusion.1 = f32[512,512]{0,1:T(8,128)} fusion(f32[4096,512]{0,1:T(8,128)} %all-reduce.7.cloned.1.call-done, f32[4096,512]{1,0:T(8,128)} %param.7), kind=kOutput, calls=%fused_computation.14 | convolution fusion | flops 12884901888 | bytes 17825792 | tf_op jit(solution)/shard_map/dot_general | solution.py:13
  457.5 14.7 %fusion.39 = f32[512,512]{1,0:T(8,128)} fusion(f32[4096,512]{0,1:T(8,128)S(1)} %copy-done.1), kind=kOutput, calls=%fused_computation.69 | convolution fusion | flops 12884901888 | bytes 9437184 | tf_op jit(solution)/shard_map/dot_general | solution.py:13
  473.4 85.3 %all-reduce.9.cloned.1.call-done = (f32[512,512]{1,0:T(8,128)}, f32[512,512]{0,1:T(8,128)}, f32[512,512]{1,0:T(8,128)}) async-done(((f32[512,512]{1,0:T(8,128)}, f32[512,512]{0,1:T(8,128)}, f32[512,512]{1,0:T(8,128)}), (f32[512,512]{1,0:T(8,128)}, f32[512,512]{0,1:T(8,128)}, f32[512,512]{1,0:T(8,128)})) %all-reduce.9.cloned.1.call-update) | async-done | bytes 3145744 | tf_op jit(solution)/shard_map/psum | solution.py:58
  562.1 3.7 fusion.5
  565.8 3.7 select_reduce_fusion
  588.0 16.7 %fusion.49 = f32[512,4096]{1,0:T(8,128)S(1)} fusion(f32[512,512]{0,1:T(8,128)} %get-tuple-element.7, f32[4096,512]{1,0:T(8,128)} %param.7), kind=kOutput, calls=%fused_computation.79 | convolution fusion | flops 12884901888 | bytes 17825792 | tf_op jit(solution)/shard_map/dot_general | solution.py:13
  604.7 7.1 fusion
  613.4 4.2 psum.70
  619.7 48.7 %all-reduce = (f32[7168]{0:T(1024)S(1)}, f32[7168]{0:T(1024)S(1)}) all-reduce(f32[7168]{0:T(1024)S(1)} %bitcast.97, f32[7168]{0:T(1024)S(1)} %bitcast.98), channel_id=1, replica_groups=mesh['dp'=16,'tensor'=2] {'dp'}, use_global_device_ids=true, to_apply=%region_17.18 | all-reduce | flops 14336 | bytes 114688 | tf_op jit(solution)/shard_map/psum | solution.py:87
  672.9 9.2 %fusion.48 = f32[1,4096]{1,0:T(1,128)S(1)} fusion(f32[512,1]{0,1:T(1,128)S(1)} %bitcast.103, f32[4096,512]{1,0:T(8,128)} %param.7), kind=kOutput, calls=%fused_computation.78 | convolution fusion | flops 25165824 | bytes 8407040 | tf_op jit(solution)/shard_map/dot_general | solution.py:13
  682.2 13.2 %fusion.2 = f32[32,7168]{1,0:T(8,128)} fusion(f32[512,7168]{1,0:T(8,128)} %all-gather.8.cloned.1.call-done, f32[32,7168]{1,0:T(8,128)S(1)} %copy-done.3, f32[7168]{0:T(1024)S(1)} %get-tuple-element.4, f32[]{:T(128)S(6)} %sin.3, f32[7168]{0:T(1024)S(1)} %get-tuple-element.5, f32[32]{0:T(128)S(1)} %dynamic-slice, f32[]{:T(128)S(6)} %sub.15, ...), kind=kOutput, calls=%fused_computation.6 | convolution fusion | flops 1411694592 | bytes 16645632 | tf_op jit(solution)/shard_map/dot_general | solution.py:13
  695.4 4.7 multiply_add_fusion
  700.1 87.7 %all-gather.6.cloned.1.call-done = f32[512,7168]{1,0:T(8,128)} async-done(((f32[32,7168]{1,0:T(8,128)}), f32[512,7168]{1,0:T(8,128)}) %all-gather.6.cloned.1.call-update) | async-done | bytes 14680080 | tf_op jit(solution)/shard_map/all_gather | solution.py:92
  787.7 12.8 %add_divide_fusion = (f32[32,7168]{1,0:T(8,128)}, f32[32,7168]{1,0:T(8,128)}) fusion(f32[32,7168]{1,0:T(8,128)} %fusion.2, f32[7168]{0:T(1024)S(1)} %get-tuple-element.4, f32[]{:T(128)S(6)} %sin.3, f32[32,7168]{1,0:T(8,128)S(1)} %copy-done.3, f32[7168]{0:T(1024)S(1)} %get-tuple-element.5, f32[32]{0:T(128)S(1)} %dynamic-slice, f32[]{:T(128)S(6)} %sub.15, ...), kind=kOutput, calls=%fused_computation.23 | convolution fusion | flops 1411907584 | bytes 18480640 | tf_op jit(solution)/shard_map/dot_general | solution.py:13
  (61 shorter events, 27.3 us)
Async XLA Ops:
  7.2 14.4 %copy-start = (bf16[128,7168]{1,0:T(8,128)(2,1)S(1)}, bf16[128,7168]{1,0:T(8,128)(2,1)}, u32[]{:S(2)}) copy-start(bf16[128,7168]{1,0:T(8,128)(2,1)} %param.6) | copy-start | bytes 5505028
  7.2 172.3 %reduce-scatter.2.cloned.1.call-start = ((), (), s32[]{:S(2)}) async-start(), calls=%async_computation.1 | async-start | bytes 15597568 | tf_op jit(solution)/shard_map/reduce_scatter | solution.py:52
  28.9 237.1 %copy-start.4 = (bf16[128,4096]{1,0:T(8,128)(2,1)S(1)}, bf16[128,4096]{1,0:T(8,128)(2,1)}, u32[]{:S(2)}) copy-start(bf16[128,4096]{1,0:T(8,128)(2,1)} %param.5) | copy-start | bytes 3145732
  28.9 221.2 %all-gather.4.cloned.1.call-start = ((), (), s32[]{:S(2)}) async-start(), calls=%async_computation.2 | async-start | bytes 7798784 | tf_op jit(solution)/shard_map/all_gather | solution.py:53
  181.5 258.6 %all-reduce.7.cloned.1.call-start = ((), (), s32[]{:S(2)}) async-start(), calls=%async_computation.3 | async-start | bytes 16777216 | tf_op jit(solution)/shard_map/psum | solution.py:57
  270.6 288.1 %all-reduce.9.cloned.1.call-start = ((), (), s32[]{:S(2)}) async-start(), calls=%async_computation.6 | async-start | bytes 6291456 | tf_op jit(solution)/shard_map/psum | solution.py:58
  440.1 17.4 %copy-start.1 = (f32[4096,512]{0,1:T(8,128)S(1)}, f32[4096,512]{0,1:T(8,128)}, u32[]{:S(2)}) copy-start(f32[4096,512]{0,1:T(8,128)} %all-reduce.7.cloned.1.call-done) | copy-start | bytes 25165828
  472.3 209.9 %all-gather.8.cloned.1.call-start = ((), (), s32[]{:S(2)}) async-start(), calls=%async_computation.5 | async-start | bytes 15597568 | tf_op jit(solution)/shard_map/all_gather | solution.py:93
  472.9 314.9 %all-gather.6.cloned.1.call-start = ((), (), s32[]{:S(2)}) async-start(), calls=%async_computation.4 | async-start | bytes 15597568 | tf_op jit(solution)/shard_map/all_gather | solution.py:92
  604.7 63.8 %copy-start.2 = (f32[512,512]{0,1:T(8,128)S(1)}, f32[512,512]{0,1:T(8,128)}, u32[]{:S(2)}) copy-start(f32[512,512]{0,1:T(8,128)} %get-tuple-element.7) | copy-start | bytes 3145732
  669.1 13.1 %copy-start.3 = (f32[32,7168]{1,0:T(8,128)S(1)}, f32[32,7168]{1,0:T(8,128)}, u32[]{:S(2)}) copy-start(f32[32,7168]{1,0:T(8,128)} %reduce-scatter.2.cloned.1.call-done) | copy-start | bytes 2752516
  682.1 13.2 %slice-start = ((s8[8388608]{0:T(1024)(128)(4,1)}), s8[4194304]{0:T(1024)(128)(4,1)S(1)}, s32[]{:S(2)}) async-start(s8[8388608]{0:T(1024)(128)(4,1)} %bitcast.95), calls=%async_computation.7 | async-start | bytes 8388608
  682.1 13.2 %slice-start.1 = ((s8[8388608]{0:T(1024)(128)(4,1)}), s8[4194304]{0:T(1024)(128)(4,1)S(1)}, s32[]{:S(2)}) async-start(s8[8388608]{0:T(1024)(128)(4,1)} %bitcast.95), calls=%async_computation.8 | async-start | bytes 8388608
Sparse Core Ops, SparseCore 0:
  29.0 150.4 reduce-scatter.1
  182.4 67.7 all-gather.3
  270.7 169.3 all-reduce.6
  472.4 86.2 all-reduce.8
  560.9 112.5 all-gather.7
  675.6 112.0 all-gather.5
where the time goes:
time: 817 us; the launch traced here: 808 us
  waiting for transfers between devices  544 us (67%)
  matrix products  157 us (19%)
  blocking collectives  73.4 us (9%)
  between operations  20.9 us (3%)
  other arithmetic  11.8 us (1%)
    psum x1, waiting for transfers between devices, body(): tangent = lax.psum(tangent_part, 'dp')  151 us
    reduce_scatter x1, waiting for transfers between devices, body(): lax.psum_scatter(grad_part, 'dp', scatter_dimension=0, tiled=True)  151 us
    dot_general x22, matrix products, matmul(): jnp.dot(left, right, precision=EXACT, preferred_element_type=jnp.float32)  133 us
    all_gather x1, waiting for transfers between devices, body(): lax.all_gather(first, 'dp', axis=0, tiled=True)  87.7 us
    psum x1, waiting for transfers between devices, body(): lax.psum((matmul(basis.T, tangent), matmul(basis.T, basis), matmul(tangen...  85.3 us
    all_gather x1, waiting for transfers between devices, body(): lax.all_gather(grad_own.astype(jnp.bfloat16), 'dp', axis=0, tiled=True)  68.6 us
    psum x1, blocking collectives, body(): along, lead_row = lax.psum((along_part, lead_part), 'dp')  48.7 us
  transfers between devices with their start and end apart: 6, of which 5 were waited for; matrix products, arithmetic and copies ran while one was open for 12% of the time, Pallas kernels for 0%

commit v1 on v0

v1 whole, which is shorter than its diff:
```python
import jax
import jax.numpy as jnp
from jax import lax
from jax.sharding import PartitionSpec as P

PI_STEPS = 6


EXACT = lax.Precision.HIGHEST


def matmul(left, right):
    return jnp.dot(left, right, precision=EXACT, preferred_element_type=jnp.float32)


def leading(normed):
    rank_count = normed.shape[0]
    vector = jnp.ones((rank_count,), jnp.float32) / jnp.sqrt(jnp.float32(rank_count))
    for sweep in range(PI_STEPS):
        vector = matmul(normed, vector)
        vector = vector / jnp.sqrt(jnp.sum(vector * vector) + 1e-12)
    return vector


def pair_sum(part, count):
    if count == 2:
        return part + lax.ppermute(part, "tensor", [(0, 1), (1, 0)])
    return lax.psum(part, "tensor")


def to_columns(block, count):
    rows, columns = block.shape
    pieces = block.reshape(rows, count, columns // count).transpose(1, 0, 2)
    pieces = lax.all_to_all(pieces, "dp", 0, 0, tiled=True)
    return pieces.reshape(count * rows, columns // count)


def body(dp, tensor, layer_inputs, out_grads, basis, first, second):
    rows_own = first.shape[0]
    rank = basis.shape[1]
    feats = basis.shape[0] // dp
    me = lax.axis_index("dp")

    grads_t = to_columns(out_grads, dp)
    basis_low = basis.astype(jnp.bfloat16)
    score_part = jnp.dot(layer_inputs, basis_low, preferred_element_type=jnp.float32)
    scores = pair_sum(score_part, tensor).astype(jnp.bfloat16)
    scores_all = lax.all_gather(scores, "dp", axis=0, tiled=True)
    inputs_t = to_columns(layer_inputs, dp)
    moments = jnp.stack([first, second]).reshape(2, rows_own, dp, -1).transpose(2, 0, 1, 3)
    moments = lax.all_to_all(moments, "dp", 0, 0, tiled=True)
    width = moments.shape[3]
    first_t = moments[:, 0].reshape(rank, width)
    second_t = moments[:, 1].reshape(rank, width)
    basis_own = lax.dynamic_slice_in_dim(basis, me * feats, feats, 0)

    grad_proj = jnp.dot(scores_all.T, grads_t, preferred_element_type=jnp.float32)
    grad_low = grad_proj.astype(jnp.bfloat16)
    back_part = jnp.dot(grads_t, grad_low.T, preferred_element_type=jnp.float32)
    back_own = lax.psum_scatter(back_part, "dp", scatter_dimension=0, tiled=True)
    backward = pair_sum(back_own, tensor).astype(jnp.bfloat16)
    back_all = lax.all_gather(backward, "dp", axis=0, tiled=True)
    tangent = jnp.dot(inputs_t.T, back_all, preferred_element_type=jnp.float32)
    correlation = lax.psum(matmul(basis_own.T, basis_own), ("dp", "tensor"))
    joint = matmul(jnp.concatenate([basis_own, tangent], axis=1).T, tangent)
    joint, correlation = lax.optimization_barrier((joint, correlation))
    joint = lax.psum(joint, ("dp", "tensor"))
    coupling, square = joint[:rank], joint[rank:]

    cross = matmul(coupling.T, 2.0 * coupling - matmul(correlation, coupling))
    kernel = square - cross
    total = jnp.trace(kernel)
    normed = kernel / total
    vector = leading(normed)
    ratio = jnp.sum(vector * matmul(normed, vector))
    theta = 4.0 * jnp.sqrt(ratio)
    sigma = jnp.sqrt(total * ratio + 1e-06)
    cos_less = jnp.cos(theta) - 1.0
    sine_val = jnp.sin(theta)
    lifted = matmul(coupling, vector)
    left_own = (matmul(tangent, vector) - matmul(basis_own, lifted)) / sigma
    left_low = left_own.astype(jnp.bfloat16)
    probe_part = jnp.dot(inputs_t, left_low, preferred_element_type=jnp.float32)
    probe = lax.psum(probe_part, ("dp", "tensor")).astype(jnp.bfloat16)
    left_part = lax.all_gather(left_own, "dp", axis=0, tiled=True)
    basis_dir = matmul(basis, vector)
    new_basis = basis + jnp.outer(cos_less * basis_dir + sine_val * left_part, vector)
    left_over = (lifted - matmul(correlation.T, lifted)) / sigma
    tilt = cos_less * matmul(correlation.T, vector) + sine_val * left_over
    rotation = correlation + jnp.outer(vector, tilt)

    along = jnp.dot(probe, grads_t, preferred_element_type=jnp.float32)
    lead_row = matmul(vector, grad_proj)
    grad_new = grad_proj + jnp.outer(vector, cos_less * lead_row + sine_val * along)
    first_new = 0.9 * matmul(rotation, first_t) + 0.1 * grad_new
    second_new = 0.95 * matmul(rotation * rotation, second_t) + 0.05 * grad_new * grad_new
    back = jnp.stack(
        [first_new.reshape(dp, rows_own, width), second_new.reshape(dp, rows_own, width)], axis=1
    )
    back = lax.all_to_all(back, "dp", 0, 0, tiled=True)
    back = back.transpose(1, 2, 0, 3).reshape(2, rows_own, dp * width)
    new_first, new_second = back[0], back[1]
    update = new_first / (jnp.sqrt(new_second) + 1e-06)
    return (new_basis, new_first, new_second, update)


def solution(mesh):
    dp, tensor = mesh.shape["dp"], mesh.shape["tensor"]

    def step(*arrays):
        return body(dp, tensor, *arrays)

    return jax.shard_map(
        step,
        mesh=mesh,
        in_specs=(
            P("dp", "tensor"),
            P("dp", "tensor"),
            P("tensor", None),
            P("dp", "tensor"),
            P("dp", "tensor"),
        ),
        out_specs=(P("tensor", None), P("dp", "tensor"), P("dp", "tensor"), P("dp", "tensor")),
        check_vma=False,
    )
```

time: 817 us -> 686 us (0.84)
  waiting for transfers between devices: 544 us -> 377 us
  matrix products: 157 us -> 58.1 us
  blocking collectives: 73.4 us -> 159 us
  local copies, waits for them, and re-layouts: 0.13 us -> 25 us
  starting transfers between devices: 0.71 us -> 21.4 us
    all_gather x3 -> x2, waiting for transfers between devices: 156 us -> 21 us  [the longest x1 21 us: body(): back_all = lax.all_gather(backward, 'dp', axis=0, tiled=True)]
    dot_general x22 -> x20, matrix products: 133 us -> 42.5 us  [matmul(): jnp.dot(left, right, precision=EXACT, preferred_element_type=jnp.float32)]
    reduce_scatter x1, waiting for transfers between devices: 151 us -> 70.3 us  [body(): lax.psum_scatter(back_part, 'dp', scatter_dimension=0, tiled=True)]
    all_to_all x0 -> x1, blocking collectives: none -> 61.8 us  [to_columns(): pieces = lax.all_to_all(pieces, 'dp', 0, 0, tiled=True)]
    all_gather x0 -> x1, blocking collectives: none -> 56.8 us  [body(): left_part = lax.all_gather(left_own, 'dp', axis=0, tiled=True)]
    psum x4 -> x1, blocking collectives: 73.4 us -> 40.5 us  [body(): probe = lax.psum(probe_part, ('dp', 'tensor')).astype(jnp.bfloat16)]
    psum x2, waiting for transfers between devices: 236 us -> 259 us  [the longest x1 135 us: body(): joint = lax.psum(joint, ('dp', 'tensor'))]
    all_to_all x0 -> x3, waiting for transfers between devices: none -> 20 us  [the longest x1 20 us: to_columns(): pieces = lax.all_to_all(pieces, 'dp', 0, 0, tiled=True)]
  transfers between devices with their start and end apart: 6 -> 10, of which waited for: 5 -> 6; matrix products, arithmetic and copies ran while one was open for 12% -> 6% of each run, Pallas kernels for 0% -> 0%
where the time goes in v1:
time: 686 us; the launch traced here: 678 us
  waiting for transfers between devices  377 us (55%)
  blocking collectives  159 us (23%)
  matrix products  58.1 us (8%)
  local copies, waits for them, and re-layouts  25 us (4%)
  between operations  22.3 us (3%)
  starting transfers between devices  21.4 us (3%)
  other arithmetic  15.4 us (2%)
    psum x1, waiting for transfers between devices, body(): joint = lax.psum(joint, ('dp', 'tensor'))  135 us
    psum x1, waiting for transfers between devices, body(): correlation = lax.psum(matmul(basis_own.T, basis_own), ('dp', 'tensor'))  125 us
    reduce_scatter x1, waiting for transfers between devices, body(): lax.psum_scatter(back_part, 'dp', scatter_dimension=0, tiled=True)  70.3 us
    all_to_all x1, blocking collectives, to_columns(): pieces = lax.all_to_all(pieces, 'dp', 0, 0, tiled=True)  61.8 us
    all_gather x1, blocking collectives, body(): left_part = lax.all_gather(left_own, 'dp', axis=0, tiled=True)  56.8 us
    dot_general x20, matrix products, matmul(): jnp.dot(left, right, precision=EXACT, preferred_element_type=jnp.float32)  42.5 us
    psum x1, blocking collectives, body(): probe = lax.psum(probe_part, ('dp', 'tensor')).astype(jnp.bfloat16)  40.5 us
    all_gather x1, waiting for transfers between devices, body(): back_all = lax.all_gather(backward, 'dp', axis=0, tiled=True)  21 us
  transfers between devices with their start and end apart: 10, of which 6 were waited for; matrix products, arithmetic and copies ran while one was open for 6% of the time, Pallas kernels for 0%

profile of v1, /device:TPU:13, one launch (start us, length us, event | category | flops | bytes accessed | tf_op | source)
XLA Modules:
  0.0 678.4 jit_solution(9894771497137540719)
XLA Ops:
  8.1 4.5 fusion
  13.9 6.0 collective-permute-done
  22.9 61.8 %all_to_all.20 = bf16[16,128,448]{1,2,0:T(8,128)(2,1)S(1)} all-to-all(bf16[16,128,448]{1,2,0:T(8,128)(2,1)} %bitcast.118), channel_id=1, replica_groups=mesh['dp'=16,'tensor'=2] {'dp'}, dimensions={0} | all-to-all | bytes 3670016 | tf_op jit(solution)/shard_map/all_to_all | solution.py:34
  84.7 3.4 fusion.5
  88.1 3.3 convolution_bitcast_fusion
  91.4 70.3 %reduce-scatter.2.cloned.1.call-done = f32[128,512]{0,1:T(8,128)} async-done(((f32[2048,512]{0,1:T(8,128)}), f32[128,512]{0,1:T(8,128)}) %reduce-scatter.2.cloned.1.call-update) | async-done | bytes 262160 | tf_op jit(solution)/shard_map/reduce_scatter | solution.py:60
  164.2 6.8 %all-to-all-start.1 = ((bf16[16,128,256]{1,2,0:T(8,128)(2,1)}), bf16[16,128,256]{1,2,0:T(8,128)(2,1)S(1)}, u32[]{:S(2)}, u32[]{:S(2)}) async-start(bf16[16,128,256]{1,2,0:T(8,128)(2,1)} %bitcast.122), calls=%async_computation.2 | async-start | bytes 2097152 | tf_op jit(solution)/shard_map/all_to_all | solution.py:34
  173.4 2.7 stack.13
  177.5 2.5 copy.45
  180.1 20.0 %all-to-all-done.1 = bf16[16,128,256]{1,2,0:T(8,128)(2,1)S(1)} async-done(((bf16[16,128,256]{1,2,0:T(8,128)(2,1)}), bf16[16,128,256]{1,2,0:T(8,128)(2,1)S(1)}, u32[]{:S(2)}, u32[]{:S(2)}) %all-to-all-start.1) | async-done | bytes 1048608 | tf_op jit(solution)/shard_map/all_to_all | solution.py:34
  200.1 4.9 all-to-all-start.2
  210.2 21.0 %all-gather.6.cloned.1.call-done = bf16[2048,512]{0,1:T(8,128)(2,1)} async-done(((bf16[128,512]{0,1:T(8,128)(2,1)}), bf16[2048,512]{0,1:T(8,128)(2,1)}) %all-gather.6.cloned.1.call-update) | async-done | bytes 2097168 | tf_op jit(solution)/shard_map/all_gather | solution.py:62
  234.3 3.2 fusion.12
  237.5 124.9 %all-reduce.3.cloned.1.call-done = f32[512,512]{1,0:T(8,128)} async-done(((f32[512,512]{1,0:T(8,128)}), f32[512,512]{1,0:T(8,128)}) %all-reduce.3.cloned.1.call-update) | async-done | bytes 1048592 | tf_op jit(solution)/shard_map/psum | solution.py:64
  362.4 3.2 fusion.41
  365.6 134.6 %all-reduce.5.cloned.1.call-done = f32[1024,512]{1,0:T(8,128)} async-done(((f32[1024,512]{1,0:T(8,128)}), f32[1024,512]{1,0:T(8,128)}) %all-reduce.5.cloned.1.call-update) | async-done | bytes 2097168 | tf_op jit(solution)/shard_map/psum | solution.py:67
  500.3 3.5 convolution_subtract_fusion.1
  532.8 40.5 %psum.23 = bf16[2048]{0:T(1024)(128)(2,1)S(1)} all-reduce(f32[2048]{0:T(1024)S(1)} %bitcast.137), channel_id=1, replica_groups=mesh['dp'=16,'tensor'=2] {'dp','tensor'}, use_global_device_ids=true, to_apply=%region_11.12 | all-reduce | flops 2048 | bytes 12288 | tf_op jit(solution)/shard_map/psum | solution.py:84
  574.5 4.4 fusion.11
  580.5 4.4 fusion.10
  588.2 7.1 %all-to-all-start.3 = ((f32[16,2,32,448]{3,2,1,0:T(8,128)}), f32[16,2,32,448]{3,2,1,0:T(8,128)S(1)}, u32[]{:S(2)}, u32[]{:S(2)}) async-start(f32[16,2,32,448]{3,2,1,0:T(8,128)} %copy.48), calls=%async_computation.4 | async-start | bytes 4194304 | tf_op jit(solution)/shard_map/all_to_all | solution.py:100
  595.2 56.8 %all-gather = f32[16,1,256]{2,1,0:T(1,128)S(1)} all-gather(f32[1,1,256]{2,1,0:T(1,128)S(1)} %bitcast.163), channel_id=1, replica_groups=mesh['dp'=16,'tensor'=2] {'dp'}, dimensions={0}, use_global_device_ids=true | all-gather | bytes 17408 | tf_op jit(solution)/shard_map/all_gather | solution.py:85
  652.0 9.3 %fusion.50 = f32[1,4096]{1,0:T(1,128)S(1)} fusion(f32[512,1]{0,1:T(1,128)S(1)} %bitcast.132, f32[4096,512]{1,0:T(8,128)} %param.7), kind=kOutput, calls=%fused_computation.86 | convolution fusion | flops 25165824 | bytes 8407040 | tf_op jit(solution)/shard_map/dot_general | solution.py:13
  661.4 6.0 multiply_add_fusion
  (104 shorter events, 50.9 us)
Async XLA Ops:
  8.0 12.6 %copy-start.13 = (bf16[128,7168]{1,0:T(8,128)(2,1)S(1)}, bf16[128,7168]{1,0:T(8,128)(2,1)}, u32[]{:S(2)}) copy-start(bf16[128,7168]{1,0:T(8,128)(2,1)} %param.6) | copy-start | bytes 5505028
  8.0 76.7 %all-gather.4.cloned.1.call-start = ((), (), s32[]{:S(2)}) async-start(), calls=%async_computation.5 | async-start | bytes 2228224 | tf_op jit(solution)/shard_map/all_gather | solution.py:48
  12.6 7.2 %collective-permute-start = (f32[128,512]{1,0:T(8,128)S(1)}, f32[128,512]{1,0:T(8,128)S(1)}, u32[]{:S(2)}, u32[]{:S(2)}) collective-permute-start(f32[128,512]{1,0:T(8,128)S(1)} %fusion), channel_id=1, source_target_pairs={{0,1},{1,0},{2,3},{3,2},{4,5},{5,4},{6,7},{7,6},{8,9},{9,8},{10,11... | collective-permute-start | bytes 786440 | tf_op jit(solution)/shard_map/ppermute | solution.py:27
  20.5 141.1 %reduce-scatter.2.cloned.1.call-start = ((), (), s32[]{:S(2)}) async-start(), calls=%async_computation.6 | async-start | bytes 4456448 | tf_op jit(solution)/shard_map/reduce_scatter | solution.py:60
  84.7 3.4 copy-start.1
  88.1 435.4 %copy-start.3 = (f32[512,448]{0,1:T(8,128)}, f32[512,448]{0,1:T(8,128)S(1)}, u32[]{:S(2)}) copy-start(f32[512,448]{0,1:T(8,128)S(1)} %fusion.5) | copy-start | bytes 2752516
  91.4 71.5 %copy-start.8 = (bf16[128,4096]{1,0:T(8,128)(2,1)S(1)}, bf16[128,4096]{1,0:T(8,128)(2,1)}, u32[]{:S(2)}) copy-start(bf16[128,4096]{1,0:T(8,128)(2,1)} %param.5) | copy-start | bytes 3145732
  161.7 9.4 %copy-start.14 = (f32[128,512]{0,1:T(8,128)S(1)}, f32[128,512]{0,1:T(8,128)}, u32[]{:S(2)}) copy-start(f32[128,512]{0,1:T(8,128)} %reduce-scatter.2.cloned.1.call-done) | copy-start | bytes 786436
  161.7 9.4 %collective-permute-start.1 = (f32[128,512]{0,1:T(8,128)}, f32[128,512]{0,1:T(8,128)S(1)}, u32[]{:S(2)}, u32[]{:S(2)}) collective-permute-start(f32[128,512]{0,1:T(8,128)} %reduce-scatter.2.cloned.1.call-done), channel_id=1, source_target_pairs={{0,1},{1,0},{2,3},{3,2},{4,5},{5,4},{6,7},{7,6},{8,9},{9,8},{10,11... | collective-permute-start | bytes 786440 | tf_op jit(solution)/shard_map/ppermute | solution.py:27
  164.2 35.9 %all-to-all-start.1 = ((bf16[16,128,256]{1,2,0:T(8,128)(2,1)}), bf16[16,128,256]{1,2,0:T(8,128)(2,1)S(1)}, u32[]{:S(2)}, u32[]{:S(2)}) async-start(bf16[16,128,256]{1,2,0:T(8,128)(2,1)} %bitcast.122), calls=%async_computation.2 | async-start | bytes 2097152 | tf_op jit(solution)/shard_map/all_to_all | solution.py:34
  171.0 60.2 %all-gather.6.cloned.1.call-start = ((), (), s32[]{:S(2)}) async-start(), calls=%async_computation.7 | async-start | bytes 2228224 | tf_op jit(solution)/shard_map/all_gather | solution.py:62
  200.1 162.3 %all-to-all-start.2 = ((f32[16,2,32,448]{3,2,1,0:T(8,128)}), f32[16,2,32,448]{3,2,1,0:T(8,128)}, u32[]{:S(2)}, u32[]{:S(2)}) async-start(f32[16,2,32,448]{3,2,1,0:T(8,128)} %copy.45), calls=%async_computation.3 | async-start | bytes 4194304 | tf_op jit(solution)/shard_map/all_to_all | solution.py:51
  205.0 157.4 %all-reduce.3.cloned.1.call-start = ((), (), s32[]{:S(2)}) async-start(), calls=%async_computation.8 | async-start | bytes 2097152 | tf_op jit(solution)/shard_map/psum | solution.py:64
  208.2 292.1 %all-reduce.5.cloned.1.call-start = ((), (), s32[]{:S(2)}) async-start(), calls=%async_computation.9 | async-start | bytes 4194304 | tf_op jit(solution)/shard_map/psum | solution.py:67
  210.2 27.3 %copy-start.9 = (bf16[16,128,256]{2,1,0:T(8,128)(2,1)}, bf16[16,128,256]{2,1,0:T(8,128)(2,1)S(1)}, u32[]{:S(2)}) copy-start(bf16[16,128,256]{2,1,0:T(8,128)(2,1)S(1)} %copy.44) | copy-start | bytes 3145732
  210.2 24.1 %copy-start.12 = (f32[256,512]{0,1:T(8,128)S(1)}, f32[256,512]{0,1:T(8,128)}, u32[]{:S(2)}) copy-start(f32[256,512]{0,1:T(8,128)} %copy.51) | copy-start | bytes 1572868
  362.4 137.9 %copy-start = (f32[512,512]{1,0:T(8,128)S(1)}, f32[512,512]{1,0:T(8,128)}, u32[]{:S(2)}) copy-start(f32[512,512]{1,0:T(8,128)} %all-reduce.3.cloned.1.call-done) | copy-start | bytes 3145732
  500.3 3.5 copy-start.7
  529.3 44.1 %copy-start.2 = (bf16[16,128,448]{1,2,0:T(8,128)(2,1)S(1)}, bf16[16,128,448]{1,2,0:T(8,128)(2,1)}, u32[]{:S(2)}) copy-start(bf16[16,128,448]{1,2,0:T(8,128)(2,1)} %copy-done.1) | copy-start | bytes 5505028
  573.3 1.2 copy-start.4
  574.5 6.0 copy-start.5
  588.2 79.2 %all-to-all-start.3 = ((f32[16,2,32,448]{3,2,1,0:T(8,128)}), f32[16,2,32,448]{3,2,1,0:T(8,128)S(1)}, u32[]{:S(2)}, u32[]{:S(2)}) async-start(f32[16,2,32,448]{3,2,1,0:T(8,128)} %copy.48), calls=%async_computation.4 | async-start | bytes 4194304 | tf_op jit(solution)/shard_map/all_to_all | solution.py:100
  668.7 2.3 copy-start.10
  669.8 1.3 copy-start.11
  (1 other events, 0.8 us)
Sparse Core Ops, SparseCore 0:
  20.7 52.4 all-gather.3
  91.5 70.1 reduce-scatter.1
  174.5 56.6 all-gather.5
Sparse Core Ops, SparseCore 1:
  210.6 151.7 all-reduce.2
  368.2 132.1 all-reduce.4

commit v2 on v1

--- a/solution.py
+++ b/solution.py
@@ -1,7 +1,14 @@
+import functools
+
 import jax
 import jax.numpy as jnp
 from jax import lax
+from jax.experimental import pallas as pl
+from jax.experimental.pallas import tpu as pltpu
 from jax.sharding import PartitionSpec as P
+
+MESH = pl.DeviceIdType.MESH
+VMEM_BYTES = 48 * 1024 * 1024
 
 PI_STEPS = 6
 
@@ -26,6 +33,156 @@
     if count == 2:
         return part + lax.ppermute(part, "tensor", [(0, 1), (1, 0)])
     return lax.psum(part, "tensor")
+
+
+def exchange_order(dp, tensor):
+    bits = lambda name, count: [(name, 1 << b) for b in range(count.bit_length() - 1)]
+    along_dp = bits("dp", dp)
+    return along_dp[:1] + bits("tensor", tensor) + along_dp[1:]
+
+
+def sum_kernel(stages, x_ref, o_ref, total, inbox, send_sem, recv_sem):
+    pieces = x_ref.shape[0]
+    place = {"dp": lax.axis_index("dp"), "tensor": lax.axis_index("tensor")}
+    sides, partners = [], []
+    for name, bit in stages:
+        side = lax.rem(place[name] // bit, 2)
+        other = dict(place)
+        other[name] = place[name] + bit * (1 - 2 * side)
+        sides.append(side)
+        partners.append((other["dp"], other["tensor"]))
+
+    barrier = pltpu.get_barrier_semaphore()
+    for partner in partners:
+        pl.semaphore_signal(barrier, inc=1, device_id=partner, device_id_type=MESH)
+    pl.semaphore_wait(barrier, len(stages))
+
+    start, base, half, slot = 0, 0, pieces, 0
+    for k, (side, partner) in enumerate(zip(sides, partners)):
+        half //= 2
+        source = x_ref if k == 0 else total
+        keep, give = start + side * half, start + (1 - side) * half
+        copy = pltpu.make_async_remote_copy(
+            src_ref=source.at[pl.ds(give, half)],
+            dst_ref=inbox.at[pl.ds(slot, half)],
+            send_sem=send_sem.at[k],
+            recv_sem=recv_sem.at[k],
+            device_id=partner,
+            device_id_type=MESH,
+        )
+        copy.start()
+        copy.wait()
+        landing = 0 if k == 0 else keep
+
+        def add(i, carry, source=source, landing=landing, keep=keep, slot=slot):
+            total[landing + i] = source[keep + i] + inbox[slot + i]
+            return carry
+
+        lax.fori_loop(0, half, add, 0)
+        base = base + side * half
+        start = landing
+        slot += half
+
+    o_ref[base] = total[start].astype(o_ref.dtype)
+    size = 1
+    for k in reversed(range(len(stages))):
+        mine = o_ref.at[pl.ds(base, size)]
+        copy = pltpu.make_async_remote_copy(
+            src_ref=mine,
+            dst_ref=mine,
+            send_sem=send_sem.at[len(stages) + k],
+            recv_sem=recv_sem.at[len(stages) + k],
+            device_id=partners[k],
+            device_id_type=MESH,
+        )
+        copy.start()
+        copy.wait()
+        base = base - sides[k] * size
+        size *= 2
+
+
+def sum_everywhere(part, kind, dp, tensor, number):
+    rows, columns = part.shape
+    count = dp * tensor
+    stages = exchange_order(dp, tensor)
+    block = (rows // count, columns)
+    out = pl.pallas_call(
+        functools.partial(sum_kernel, stages),
+        out_shape=jax.ShapeDtypeStruct((count, *block), kind),
+        in_specs=[pl.BlockSpec(memory_space=pltpu.VMEM)],
+        out_specs=pl.BlockSpec(memory_space=pltpu.VMEM),
+        scratch_shapes=[
+            pltpu.VMEM((count // 2, *block), jnp.float32),
+            pltpu.VMEM((count - 1, *block), jnp.float32),
+            pltpu.SemaphoreType.DMA((2 * len(stages),)),
+            pltpu.SemaphoreType.DMA((2 * len(stages),)),
+        ],
+        compiler_params=pltpu.CompilerParams(
+            collective_id=number, has_side_effects=True, vmem_limit_bytes=VMEM_BYTES
+        ),
+    )(part.reshape(count, *block))
+    return out.reshape(rows, columns)
+
+
+def spread_kernel(dp, tensor, x_ref, o_ref, send_sem, recv_sem):
+    count = dp * tensor
+    me = lax.axis_index("dp") * tensor + lax.axis_index("tensor")
+
+    def device(index):
+        return (index // tensor, lax.rem(index, tensor))
+
+    barrier = pltpu.get_barrier_semaphore()
+
+    def greet(step, carry):
+        pl.semaphore_signal(
+            barrier, inc=1, device_id=device(lax.rem(me + step, count)), device_id_type=MESH
+        )
+        return carry
+
+    lax.fori_loop(1, count, greet, 0)
+    pl.semaphore_wait(barrier, count - 1)
+
+    def copy(step, place):
+        return pltpu.make_async_remote_copy(
+            src_ref=x_ref,
+            dst_ref=o_ref.at[place],
+            send_sem=send_sem.at[step],
+            recv_sem=recv_sem.at[step],
+            device_id=device(lax.rem(me + step, count)),
+            device_id_type=MESH,
+        )
+
+    def send(step, carry):
+        copy(step, me).start()
+        return carry
+
+    def land(step, carry):
+        copy(step, lax.rem(me + count - step, count)).wait()
+        return carry
+
+    lax.fori_loop(1, count, send, 0)
+    o_ref[me] = x_ref[...]
+    lax.fori_loop(1, count, land, 0)
+
+
+def spread(vector, dp, tensor, number):
+    count, length = dp * tensor, vector.shape[0]
+    rows = -(-length // 1024) * 8
+    block = jnp.pad(vector, (0, rows * 128 - length)).reshape(rows, 128)
+    out = pl.pallas_call(
+        functools.partial(spread_kernel, dp, tensor),
+        out_shape=jax.ShapeDtypeStruct((count, rows, 128), jnp.float32),
+        in_specs=[pl.BlockSpec(memory_space=pltpu.VMEM)],
+        out_specs=pl.BlockSpec(memory_space=pltpu.VMEM),
+        scratch_shapes=[
+            pltpu.SemaphoreType.DMA((count,)),
+            pltpu.SemaphoreType.DMA((count,)),
+        ],
+        compiler_params=pltpu.CompilerParams(
+            collective_id=number, has_side_effects=True, vmem_limit_bytes=VMEM_BYTES
+        ),
+    )(block)
+    return out.reshape(dp, tensor, rows * 128)
 
 
 def to_columns(block, count):
@@ -57,14 +214,11 @@
     grad_proj = jnp.dot(scores_all.T, grads_t, preferred_element_type=jnp.float32)
     grad_low = grad_proj.astype(jnp.bfloat16)
     back_part = jnp.dot(grads_t, grad_low.T, preferred_element_type=jnp.float32)
-    back_own = lax.psum_scatter(back_part, "dp", scatter_dimension=0, tiled=True)
-    backward = pair_sum(back_own, tensor).astype(jnp.bfloat16)
-    back_all = lax.all_gather(backward, "dp", axis=0, tiled=True)
+    back_all = sum_everywhere(back_part, jnp.bfloat16, dp, tensor, 0)
     tangent = jnp.dot(inputs_t.T, back_all, preferred_element_type=jnp.float32)
-    correlation = lax.psum(matmul(basis_own.T, basis_own), ("dp", "tensor"))
+    correlation = pair_sum(matmul(basis.T, basis), tensor)
     joint = matmul(jnp.concatenate([basis_own, tangent], axis=1).T, tangent)
-    joint, correlation = lax.optimization_barrier((joint, correlation))
-    joint = lax.psum(joint, ("dp", "tensor"))
+    joint = sum_everywhere(joint, jnp.float32, dp, tensor, 1)
     coupling, square = joint[:rank], joint[rank:]
 
     cross = matmul(coupling.T, 2.0 * coupling - matmul(correlation, coupling))
@@ -81,8 +235,11 @@
     left_own = (matmul(tangent, vector) - matmul(basis_own, lifted)) / sigma
     left_low = left_own.astype(jnp.bfloat16)
     probe_part = jnp.dot(inputs_t, left_low, preferred_element_type=jnp.float32)
-    probe = lax.psum(probe_part, ("dp", "tensor")).astype(jnp.bfloat16)
-    left_part = lax.all_gather(left_own, "dp", axis=0, tiled=True)
+    tokens = probe_part.shape[0]
+    parts = spread(jnp.concatenate([probe_part, left_own]), dp, tensor, 2)
+    probe = jnp.sum(parts[:, :, :tokens], axis=(0, 1)).astype(jnp.bfloat16)
+    left_part = lax.dynamic_index_in_dim(parts, lax.axis_index("tensor"), 1, keepdims=False)
+    left_part = left_part[:, tokens : tokens + feats].reshape(-1)
     basis_dir = matmul(basis, vector)
     new_basis = basis + jnp.outer(cos_less * basis_dir + sine_val * left_part, vector)
     left_over = (lifted - matmul(correlation.T, lifted)) / sigma

time: 686 us -> 451 us (0.66)
  waiting for transfers between devices: 377 us -> 118 us
  blocking collectives: 159 us -> 0 us
  Pallas kernels: 0 us -> 158 us
  local copies, waits for them, and re-layouts: 25 us -> 36.9 us
  matrix products: 58.1 us -> 69.5 us
    psum x2 -> x0, waiting for transfers between devices: 259 us -> none  [the longest x1 135 us: body(): joint = lax.psum(joint, ('dp', 'tensor'))]
    pallas_call x0 -> x3, Pallas kernels: none -> 158 us  [the longest x2 143 us: sum_everywhere(): pl.pallas_call(functools.partial(sum_kernel, stages), out_shape=jax.Shape...]
    reduce_scatter x1 -> x0, waiting for transfers between devices: 70.3 us -> none  [body(): lax.psum_scatter(back_part, 'dp', scatter_dimension=0, tiled=True)]
    all_to_all x1 -> x0, blocking collectives: 61.8 us -> none  [to_columns(): pieces = lax.all_to_all(pieces, 'dp', 0, 0, tiled=True)]
    all_gather x1 -> x0, blocking collectives: 56.8 us -> none  [body(): left_part = lax.all_gather(left_own, 'dp', axis=0, tiled=True)]
    psum x1 -> x0, blocking collectives: 40.5 us -> none  [body(): probe = lax.psum(probe_part, ('dp', 'tensor')).astype(jnp.bfloat16)]
    all_to_all x1, waiting for transfers between devices: 0.01 us -> 38.5 us  [body(): moments = lax.all_to_all(moments, 'dp', 0, 0, tiled=True)]
    all_to_all x1, waiting for transfers between devices: 0.01 us -> 31.9 us  [body(): back = lax.all_to_all(back, 'dp', 0, 0, tiled=True)]
  transfers between devices with their start and end apart: 10 -> 7, of which waited for: 6 -> 5; matrix products, arithmetic and copies ran while one was open for 6% -> 12% of each run, Pallas kernels for 0% -> 0%
where the time goes in v2:
time: 451 us; the launch traced here: 446 us
  Pallas kernels  158 us (35%)
  waiting for transfers between devices  118 us (26%)
  matrix products  69.5 us (15%)
  local copies, waits for them, and re-layouts  36.9 us (8%)
  starting transfers between devices  25.5 us (6%)
  between operations  21.3 us (5%)
  other arithmetic  16.7 us (4%)
    pallas_call x2, Pallas kernels, sum_everywhere(): pl.pallas_call(functools.partial(sum_kernel, stages), out_shape=jax.Shape...  143 us
    dot_general x20, matrix products, matmul(): jnp.dot(left, right, precision=EXACT, preferred_element_type=jnp.float32)  55.8 us
    all_to_all x1, waiting for transfers between devices, body(): moments = lax.all_to_all(moments, 'dp', 0, 0, tiled=True)  38.5 us
    all_to_all x1, waiting for transfers between devices, body(): back = lax.all_to_all(back, 'dp', 0, 0, tiled=True)  31.9 us
    ppermute x2, waiting for transfers between devices, pair_sum(): return part + lax.ppermute(part, 'tensor', [(0, 1), (1, 0)])  28.1 us
    all_to_all x2, waiting for transfers between devices, to_columns(): pieces = lax.all_to_all(pieces, 'dp', 0, 0, tiled=True)  19.9 us
    pallas_call x1, Pallas kernels, spread(): pl.pallas_call(functools.partial(spread_kernel, dp, tensor), out_shape=ja...  14.8 us
    unnamed x40, local copies, waits for them, and re-layouts  12.2 us
  transfers between devices with their start and end apart: 7, of which 5 were waited for; matrix products, arithmetic and copies ran while one was open for 12% of the time, Pallas kernels for 0%

profile of v2, /device:TPU:13, one launch (start us, length us, event | category | flops | bytes accessed | tf_op | source)
XLA Modules:
  0.0 446.1 jit_solution(9937217866015830474)
XLA Ops:
  9.5 6.6 %all-to-all-start.1 = ((bf16[16,128,256]{1,2,0:T(8,128)(2,1)}), bf16[16,128,256]{1,2,0:T(8,128)(2,1)S(1)}, u32[]{:S(2)}, u32[]{:S(2)}) async-start(bf16[16,128,256]{1,2,0:T(8,128)(2,1)} %bitcast.6), calls=%async_computation.1 | async-start | bytes 2097152 | tf_op jit(solution)/shard_map/all_to_all | solution.py:191
  18.5 2.5 copy.50
  21.0 19.9 %all-to-all-done.1 = bf16[16,128,256]{1,2,0:T(8,128)(2,1)S(1)} async-done(((bf16[16,128,256]{1,2,0:T(8,128)(2,1)}), bf16[16,128,256]{1,2,0:T(8,128)(2,1)S(1)}, u32[]{:S(2)}, u32[]{:S(2)}) %all-to-all-start.1) | async-done | bytes 1048608 | tf_op jit(solution)/shard_map/all_to_all | solution.py:191
  41.9 4.9 %all-to-all-start.2 = ((f32[16,2,32,448]{3,2,1,0:T(8,128)}), f32[16,2,32,448]{3,2,1,0:T(8,128)S(1)}, u32[]{:S(2)}, u32[]{:S(2)}) async-start(f32[16,2,32,448]{3,2,1,0:T(8,128)} %copy.50), calls=%async_computation.2 | async-start | bytes 4194304 | tf_op jit(solution)/shard_map/all_to_all | solution.py:208
  46.9 4.1 fusion
  52.3 6.3 %collective-permute-done = f32[128,512]{1,0:T(8,128)S(1)} collective-permute-done((f32[128,512]{1,0:T(8,128)S(1)}, f32[128,512]{1,0:T(8,128)S(1)}, u32[]{:S(2)}, u32[]{:S(2)}) %collective-permute-start) | collective-permute-done | bytes 262176 | tf_op jit(solution)/shard_map/ppermute | solution.py:34
  59.3 3.9 copy.45
  63.2 38.5 %all-to-all-done.2 = f32[16,2,32,448]{3,2,1,0:T(8,128)S(1)} async-done(((f32[16,2,32,448]{3,2,1,0:T(8,128)}), f32[16,2,32,448]{3,2,1,0:T(8,128)S(1)}, u32[]{:S(2)}, u32[]{:S(2)}) %all-to-all-start.2) | async-done | bytes 1835040 | tf_op jit(solution)/shard_map/all_to_all | solution.py:208
  103.1 5.2 %all-to-all-start = ((bf16[16,128,448]{1,2,0:T(8,128)(2,1)}), bf16[16,128,448]{1,2,0:T(8,128)(2,1)S(1)}, u32[]{:S(2)}, u32[]{:S(2)}) async-start(bf16[16,128,448]{1,2,0:T(8,128)(2,1)} %bitcast.139), calls=%async_computation | async-start | bytes 3670016 | tf_op jit(solution)/shard_map/all_to_all | solution.py:191
  108.3 18.2 %fusion.42 = f32[512,512]{1,0:T(8,128)} fusion(f32[4096,512]{1,0:T(8,128)} %param.7), kind=kOutput, calls=%fused_computation.82 | convolution fusion | flops 12884901888 | bytes 9437184 | tf_op jit(solution)/shard_map/dot_general | solution.py:20
  129.5 21.7 %collective-permute-done.1 = f32[512,512]{1,0:T(8,128)} collective-permute-done((f32[512,512]{1,0:T(8,128)}, f32[512,512]{1,0:T(8,128)}, u32[]{:S(2)}, u32[]{:S(2)}) %collective-permute-start.1) | collective-permute-done | bytes 1048608 | tf_op jit(solution)/shard_map/ppermute | solution.py:34
  155.2 3.2 fusion.39
  158.5 3.4 fusion.5
  162.8 3.3 convolution_bitcast_fusion
  166.1 5.3 %copy.47 = f32[2048,512]{1,0:T(8,128)} copy(f32[2048,512]{0,1:T(8,128)} %convolution_bitcast_fusion) | data formatting | bytes 8388608 | tf_op jit(solution)/shard_map/dot_general | solution.py:216
  171.4 85.4 %shard_map.84 = bf16[32,64,512]{2,1,0:T(8,128)(2,1)S(1)} custom-call(f32[32,64,512]{2,1,0:T(8,128)} %bitcast.134), custom_call_target="tpu_custom_call" | custom-call | tf_op jit(solution)/shard_map/pallas_call | solution.py:109
  259.4 57.8 %shard_map.85 = f32[32,32,512]{2,1,0:T(8,128)S(1)} custom-call(f32[32,32,512]{2,1,0:T(8,128)S(1)} %bitcast.130), custom_call_target="tpu_custom_call" | custom-call | tf_op jit(solution)/shard_map/pallas_call | solution.py:109
  349.0 14.8 %shard_map.86 = f32[32,24,128]{2,1,0:T(8,128)S(1)} custom-call(f32[24,128]{1,0:T(8,128)S(1)} %fusion.27.x_ref), custom_call_target="tpu_custom_call" | custom-call | tf_op jit(solution)/shard_map/pallas_call | solution.py:172
  366.9 4.4 fusion.11
  372.9 4.4 fusion.10
  380.6 6.4 %all-to-all-start.3 = ((f32[16,2,32,448]{3,2,1,0:T(8,128)}), f32[16,2,32,448]{3,2,1,0:T(8,128)S(1)}, u32[]{:S(2)}, u32[]{:S(2)}) async-start(f32[16,2,32,448]{3,2,1,0:T(8,128)} %copy.53), calls=%async_computation.3 | async-start | bytes 4194304 | tf_op jit(solution)/shard_map/all_to_all | solution.py:257
  387.2 9.2 %fusion.49 = f32[1,4096]{1,0:T(1,128)S(1)} fusion(f32[512,1]{0,1:T(1,128)S(1)} %bitcast.151, f32[4096,512]{1,0:T(8,128)} %param.7), kind=kOutput, calls=%fused_computation.89 | convolution fusion | flops 25165824 | bytes 8407040 | tf_op jit(solution)/shard_map/dot_general | solution.py:20
  396.4 6.0 %multiply_add_fusion = f32[4096,512]{1,0:T(8,128)} fusion(f32[4096,512]{1,0:T(8,128)} %param.7, f32[512]{0:T(512)S(1)} %broadcast_divide_fusion.1, f32[4096]{0:T(1024)S(1)} %multiply_add_fusion.5), kind=kLoop, calls=%fused_computation | loop fusion | flops 4194304 | bytes 16795648 | tf_op jit(solution)/shard_map/add | solution.py:244
  402.4 31.9 %all-to-all-done.3 = f32[16,2,32,448]{3,2,1,0:T(8,128)S(1)} async-done(((f32[16,2,32,448]{3,2,1,0:T(8,128)}), f32[16,2,32,448]{3,2,1,0:T(8,128)S(1)}, u32[]{:S(2)}, u32[]{:S(2)}) %all-to-all-start.3) | async-done | bytes 1835040 | tf_op jit(solution)/shard_map/all_to_all | solution.py:257
  (106 shorter events, 57.5 us)
Async XLA Ops:
  7.2 8.9 %copy-start.16 = (f32[32,7168]{1,0:T(8,128)S(1)}, f32[32,7168]{1,0:T(8,128)}, u32[]{:S(2)}) copy-start(f32[32,7168]{1,0:T(8,128)} %param.8) | copy-start | bytes 2752516
  9.5 31.4 %all-to-all-start.1 = ((bf16[16,128,256]{1,2,0:T(8,128)(2,1)}), bf16[16,128,256]{1,2,0:T(8,128)(2,1)S(1)}, u32[]{:S(2)}, u32[]{:S(2)}) async-start(bf16[16,128,256]{1,2,0:T(8,128)(2,1)} %bitcast.6), calls=%async_computation.1 | async-start | bytes 2097152 | tf_op jit(solution)/shard_map/all_to_all | solution.py:191
  21.0 25.9 %copy-start.10 = (bf16[128,4096]{1,0:T(8,128)(2,1)S(1)}, bf16[128,4096]{1,0:T(8,128)(2,1)}, u32[]{:S(2)}) copy-start(bf16[128,4096]{1,0:T(8,128)(2,1)} %param.5) | copy-start | bytes 3145732
  41.0 1.0 copy-start.11
  41.9 59.8 %all-to-all-start.2 = ((f32[16,2,32,448]{3,2,1,0:T(8,128)}), f32[16,2,32,448]{3,2,1,0:T(8,128)S(1)}, u32[]{:S(2)}, u32[]{:S(2)}) async-start(f32[16,2,32,448]{3,2,1,0:T(8,128)} %copy.50), calls=%async_computation.2 | async-start | bytes 4194304 | tf_op jit(solution)/shard_map/all_to_all | solution.py:208
  46.9 111.6 %all-gather.2.cloned.1.call-start = ((), (), s32[]{:S(2)}) async-start(), calls=%async_computation.4 | async-start | bytes 2228224 | tf_op jit(solution)/shard_map/all_gather | solution.py:205
  51.0 7.6 %collective-permute-start = (f32[128,512]{1,0:T(8,128)S(1)}, f32[128,512]{1,0:T(8,128)S(1)}, u32[]{:S(2)}, u32[]{:S(2)}) collective-permute-start(f32[128,512]{1,0:T(8,128)S(1)} %fusion), channel_id=1, source_target_pairs={{0,1},{1,0},{2,3},{3,2},{4,5},{5,4},{6,7},{7,6},{8,9},{9,8},{10,11... | collective-permute-start | bytes 786440 | tf_op jit(solution)/shard_map/ppermute | solution.py:34
  101.7 1.3 copy-start.8
  103.1 55.4 %all-to-all-start = ((bf16[16,128,448]{1,2,0:T(8,128)(2,1)}), bf16[16,128,448]{1,2,0:T(8,128)(2,1)S(1)}, u32[]{:S(2)}, u32[]{:S(2)}) async-start(bf16[16,128,448]{1,2,0:T(8,128)(2,1)} %bitcast.139), calls=%async_computation | async-start | bytes 3670016 | tf_op jit(solution)/shard_map/all_to_all | solution.py:191
  126.5 24.7 %collective-permute-start.1 = (f32[512,512]{1,0:T(8,128)}, f32[512,512]{1,0:T(8,128)}, u32[]{:S(2)}, u32[]{:S(2)}) collective-permute-start(f32[512,512]{1,0:T(8,128)} %fusion.42), channel_id=1, source_target_pairs={{0,1},{1,0},{2,3},{3,2},{4,5},{5,4},{6,7},{7,6},{8,9},{9,8},{10,11... | collective-permute-start | bytes 3145736 | tf_op jit(solution)/shard_map/ppermute | solution.py:34
  128.7 0.8 copy-start.9
  158.4 3.4 copy-start
  161.8 0.9 copy-start.2
  171.4 85.4 %copy-start.5 = (bf16[16,128,256]{2,1,0:T(8,128)(2,1)S(1)}, bf16[16,128,256]{2,1,0:T(8,128)(2,1)}, u32[]{:S(2)}) copy-start(bf16[16,128,256]{2,1,0:T(8,128)(2,1)} %copy.49) | copy-start | bytes 3145732
  257.6 1.9 copy-start.6
  337.0 3.1 copy-start.7
  345.7 20.0 %copy-start.1 = (bf16[16,128,448]{1,2,0:T(8,128)(2,1)S(1)}, bf16[16,128,448]{1,2,0:T(8,128)(2,1)}, u32[]{:S(2)}) copy-start(bf16[16,128,448]{1,2,0:T(8,128)(2,1)} %copy-done) | copy-start | bytes 5505028
  365.8 1.2 copy-start.3
  366.9 6.0 %copy-start.4 = (f32[512,448]{0,1:T(8,128)S(1)}, f32[512,448]{0,1:T(8,128)}, u32[]{:S(2)}) copy-start(f32[512,448]{0,1:T(8,128)} %copy-done.2) | copy-start | bytes 2752516
  380.6 6.4 %copy-start.15 = (f32[16,2,3072]{2,1,0:T(2,128)S(1)}, f32[16,2,3072]{2,1,0:T(2,128)}, u32[]{:S(2)}) copy-start(f32[16,2,3072]{2,1,0:T(2,128)} %reshape.64) | copy-start | bytes 1179652
  380.6 53.7 %all-to-all-start.3 = ((f32[16,2,32,448]{3,2,1,0:T(8,128)}), f32[16,2,32,448]{3,2,1,0:T(8,128)S(1)}, u32[]{:S(2)}, u32[]{:S(2)}) async-start(f32[16,2,32,448]{3,2,1,0:T(8,128)} %copy.53), calls=%async_computation.3 | async-start | bytes 4194304 | tf_op jit(solution)/shard_map/all_to_all | solution.py:257
  435.4 1.2 copy-start.12
  436.5 2.5 copy-start.13
  437.7 1.3 copy-start.14
Sparse Core Ops, SparseCore 0:
  59.5 52.3 all-gather.1
